TPU v7x, 128 devices: a whole 4x4x4 slice. The times are simulated.
128 devices in a mesh: space: 16 (over y_hi, z, core), spec: 8 (over y_lo, x).
Axes of the slice: x: 4, y: 4 (y_hi: 2, y_lo: 2; y = y_hi * 2 + y_lo), z: 4, core: 2. Of those that a mesh axis runs over, the one named last changes fastest.
Arguments:
- spectrum: float32 [1296, 128, 128], P('spec', 'space'), may hold values from -6 to 6
- ocean_mask: int32 [128, 128], P('space'), may hold values 0 or 1
- depth_class: int32 [128, 128], P('space'), may hold values from 0 to 7
- freq_speed: float32 [36], replicated, may hold values from 0.15 to 0.45
- coupling: bfloat16 [1296, 1296], replicated, may hold values from -0.0390625 to 0.0390625
- source: bfloat16 [1296, 1296], replicated, may hold values from -0.0390625 to 0.0390625
- gain_table: float32 [8, 1296], replicated, may hold values from 0.5 to 2
Outputs:
- result: float32 [1296, 128, 128], P('spec', 'space')
All inputs are finite; a program needn't handle non-finite values. No bound on the sum of `ocean_mask` on one device may be relied on, other than what follows from the above.
Results may differ from a plain program's by a relative error of at most 0.00088.
Values sent between devices are 32-bit elements; how exact they have to be, the bound alone decides.
A program may use at most 64 MiB of HBM per device.

v0:
```python
import functools
import math

import jax
import jax.numpy as jnp
from jax import lax
from jax.experimental import pallas as pl
from jax.experimental.pallas import tpu as pltpu
from jax.sharding import PartitionSpec as P

MESH = pl.DeviceIdType.MESH
F32, BF16, I32 = jnp.float32, jnp.bfloat16, jnp.int32
BINS, NDIR, NFREQ, CLASSES = 1296, 36, 36, 8
ITERS = 4
NSPEC, LOCAL = 8, 162
SLOT = 48
FULL = (5, 5, 4, 4)
BASE = (0, 48, 96, 136)
KEPT = (48, 48, 40, 40)
ROWS = 176
LOWX, LOWY = (True, False, False, True), (True, True, False, False)
PAIRS = ((0, 0), (1, 0), (1, 1), (2, 1), (3, 1), (3, 2), (4, 2), (5, 2))
PHASES = ITERS + 1


def off_j(q):
    return 4 if LOWY[q] else 0


def off_i(q):
    return 8 if LOWX[q] else 0


def block_of(r, half):
    low = lax.rem(r // 4 + half, 2)
    x = lax.rem(r, 4)
    return jnp.where(low == 0, x, 7 - x)


def owner_of(c, half):
    x = jnp.where(c < 4, c, 7 - c)
    return lax.rem(c // 4 + half, 2) * 4 + x


def swap_blocks(parts):
    lane = lax.broadcasted_iota(I32, parts[0].shape, 1)
    for h in (4, 2, 1):
        keep = (lane & (16 * h)) == 0
        new = list(parts)
        for j in range(8):
            if j & h == 0:
                a, b = parts[j], parts[j + h]
                new[j] = jnp.where(keep, a, pltpu.roll(b, 16 * h, 1))
                new[j + h] = jnp.where(keep, pltpu.roll(a, 128 - 16 * h, 1), b)
        parts = new
    return parts


def local_bin(rel, idx):
    many = rel < 2
    whole = jnp.where(many, 40, 32)
    runs = jnp.where(many, 5, 4)
    first = 36 * (idx >> 3) + (idx & 7)
    last = 36 * (idx - whole) + 8
    return jnp.where(idx < whole, first + 9 * rel, jnp.where(idx < whole + runs, last + 9 * rel, -10000))


def places(q, g, shape):
    slot = 128 * g + lax.broadcasted_iota(I32, shape, len(shape) - 1)
    r = jnp.zeros_like(slot)
    for k in range(1, 8):
        r = r + (slot >= SLOT * k).astype(I32)
    return r, q ^ (2 * (r & 1)), slot - SLOT * r


def kernel(ns, x_ref, mask_ref, class_ref, speed_ref, coupling_ref, source_ref, gain_ref, out_ref,
           natural, turned, weights, pick, e0, e1, slope, xb, yb, gains, gain_rows, mask, coef,
           send_a, land_a, land_b, xs, cs, yl, xl, cl, tile, strip, mask_own, mask_land,
           w_sem, a_send, a_recv, b_send, b_recv, h_send, h_recv, m_send, m_recv):
    r = lax.axis_index("spec")
    s = lax.axis_index("space")
    half = s // (ns // 2)
    c = block_of(r, half)

    def at(dc, ds):
        cc, ss = jnp.clip(c + dc, 0, NSPEC - 1), jnp.clip(s + ds, 0, ns - 1)
        return (ss, owner_of(cc, ss // (ns // 2)))

    def there(dc, ds):
        ok = None
        for cond in ([c + dc >= 0, c + dc < NSPEC] if dc else []) + ([s + ds >= 0, s + ds < ns] if ds else []):
            ok = cond if ok is None else jnp.logical_and(ok, cond)
        return ok

    loads = [pltpu.make_async_copy(ref, natural.at[m], w_sem.at[m]) for m, ref in enumerate((coupling_ref, source_ref))]
    for copy in loads:
        copy.start()
    barrier = pltpu.get_barrier_semaphore()
    around = [(dc, ds) for ds in (-1, 1) for dc in (-1, 0, 1)]
    for k in range(1, NSPEC):
        pl.semaphore_signal(barrier, inc=1, device_id=(s, lax.rem(r + k, NSPEC)), device_id_type=MESH)
    for dc, ds in around:
        @pl.when(there(dc, ds))
        def _():
            pl.semaphore_signal(barrier, inc=1, device_id=at(dc, ds), device_id_type=MESH)

    mask_own[...] = mask_ref[...].astype(F32)

    for rel in range(4):
        def pack(f, _, rel=rel):
            parts = [x_ref[pl.ds((36 * f + 9 * rel) * 8 + j, 8, stride=8), :] for j in range(8)]
            for cc, part in enumerate(swap_blocks(parts)):
                send_a[cc, pl.ds(pl.multiple_of(BASE[rel] + 8 * f, 8), 8), :] = part
            return 0
        lax.fori_loop(0, FULL[rel], pack, 0)
        n = FULL[rel]
        parts = [x_ref[pl.ds((9 * rel + 8) * 8 + j, n, stride=288), :] for j in range(8)]
        for cc, part in enumerate(swap_blocks(parts)):
            send_a[cc, BASE[rel] + 8 * n:BASE[rel] + 8 * n + 8, :] = jnp.zeros((8, 128), F32)
            send_a[cc, BASE[rel] + 8 * n:BASE[rel] + 9 * n, :] = part

    beside = (c > 0).astype(I32) + (c < NSPEC - 1).astype(I32)
    beyond = (s > 0).astype(I32) + (s < ns - 1).astype(I32)
    pl.semaphore_wait(barrier, NSPEC - 1 + beyond * (1 + beside))

    def a_copy(k, incoming=False):
        peer = lax.rem(r + k, NSPEC)
        return pltpu.make_async_remote_copy(
            src_ref=send_a.at[block_of(peer, half)], dst_ref=land_a.at[peer if incoming else r],
            send_sem=a_send.at[k], recv_sem=a_recv.at[peer if incoming else r],
            device_id=(s, peer), device_id_type=MESH)

    for k in range(1, NSPEC):
        a_copy(k).start()
    own_a = pltpu.make_async_copy(send_a.at[c], land_a.at[r], a_send.at[0])
    own_a.start()

    def mask_copy(ds, incoming=False):
        k = (1 if ds < 0 else 0) if not incoming else (0 if ds < 0 else 1)
        return pltpu.make_async_remote_copy(
            src_ref=mask_own, dst_ref=mask_land.at[k], send_sem=m_send.at[k], recv_sem=m_recv.at[k],
            device_id=at(0, ds), device_id_type=MESH)

    for ds in (-1, 1):
        @pl.when(there(0, ds))
        def _():
            mask_copy(ds).start()

    def clear(qg, _):
        e0[qg] = jnp.zeros((12, 24, 128), F32)
        e1[qg] = jnp.zeros((12, 24, 128), F32)
        return 0
    lax.fori_loop(0, 12, clear, 0)

    row = lax.broadcasted_iota(I32, (16, 128), 0)
    quad = (row >= 3).astype(I32) + (row >= 6).astype(I32) + (row >= 9).astype(I32)
    home, rel, idx = places(quad, row - 3 * quad, (16, 128))
    here = local_bin(rel, idx)
    many = rel < 2
    whole = jnp.where(many, 40, 32)
    run = jnp.where(idx < whole, idx >> 3, idx - whole)
    step = jnp.where(idx < whole, idx & 7, 8)
    freq = ((9 * home) >> 1) + run + jnp.where(many, 0, home & 1)
    group_speed = jnp.zeros((16, 128), F32)
    for k in range(NFREQ):
        group_speed = jnp.where(freq == k, speed_ref[k], group_speed)
    group_speed = jnp.where(here >= 0, group_speed, 0.0)
    cosine, sine = jnp.zeros((16, 128), F32), jnp.zeros((16, 128), F32)
    for k in range(9):
        cosine = jnp.where(step == k, math.cos(2.0 * math.pi * (k + 0.5) / NDIR), cosine)
        sine = jnp.where(step == k, math.sin(2.0 * math.pi * (k + 0.5) / NDIR), sine)
    even = (quad & 1) == 0
    ax = group_speed * jnp.where(even, cosine, sine)
    ay = group_speed * jnp.where(even, sine, cosine)
    coef[0] = 1.0 - ax - ay
    coef[1] = ax
    coef[2] = ay

    for k, (t, g) in enumerate(PAIRS):
        rows = 16 if t == 5 else 256
        for q in range(4):
            home, rel, idx = places(jnp.full((1, 128), q, I32), g, (1, 128))
            want = LOCAL * home + local_bin(rel, idx) - 256 * t
            hit = lax.broadcasted_iota(I32, (rows, 128), 0) == want
            pick[k, 0:rows, 128 * q:128 * q + 128] = jnp.where(hit, 1.0, 0.0).astype(BF16)

    def to_quadrants(lhs, g):
        total = None
        for k, (t, gg) in enumerate(PAIRS):
            if gg == g:
                rows = 16 if t == 5 else 256
                term = jnp.dot(lhs(256 * t, rows), pick[k, 0:rows, :], preferred_element_type=F32)
                total = term if total is None else total + term
        return total

    table = gain_ref[...]
    high = table.astype(BF16).astype(F32)
    mid = (table - high).astype(BF16).astype(F32)
    low = table - high - mid
    thirds = jnp.concatenate([high, mid, low, jnp.zeros_like(low)], axis=0).astype(BF16)
    for g in range(3):
        total = to_quadrants(lambda at_, n: thirds[:, at_:at_ + n], g)
        for q in range(4):
            part = total[:, 128 * q:128 * q + 128]
            gain_rows[3 * q + g] = part[0:8] + part[8:16] + part[16:24]

    for copy in loads:
        copy.wait()
    for m in range(2):
        def columns(k, _, m=m):
            rows = pl.ds(pl.multiple_of(144 * k, 16), 144)
            for g in range(3):
                total = to_quadrants(lambda at_, n: natural[m, rows, at_:at_ + n], g).astype(BF16)
                for q in range(4):
                    turned[3 * q + g, rows, 128 * m:128 * m + 128] = total[:, 128 * q:128 * q + 128]
            return 0
        lax.fori_loop(0, 9, columns, 0)

    for rr in range(NSPEC):
        blocks = []
        for q in range(4):
            place = lax.broadcasted_iota(I32, (SLOT, 176), 0)
            want = local_bin(jnp.full((SLOT, 176), q ^ (2 * (rr & 1)), I32), place) + 2 * rr
            hit = lax.broadcasted_iota(I32, (SLOT, 176), 1) == want
            blocks.append(jnp.where(hit, 1.0, 0.0).astype(BF16))
        onehot = jnp.concatenate(blocks, axis=0)

        def lines(qg, _, rr=rr, onehot=onehot):
            got = jnp.dot(onehot, turned[qg, 160 * rr:160 * rr + 176, :], preferred_element_type=F32).astype(BF16)
            for q in range(4):
                weights[qg, 384 * q + SLOT * rr:384 * q + SLOT * rr + SLOT, :] = got[SLOT * q:SLOT * q + SLOT]
            return 0
        lax.fori_loop(0, 12, lines, 0, unroll=2)

    for k, ds in ((0, -1), (1, 1)):
        @pl.when(there(0, ds))
        def _():
            mask_copy(ds, incoming=True).wait_recv()
            mask_copy(ds).wait_send()
            tile[16 * k:16 * k + 8, :] = mask_land[k]

        @pl.when(jnp.logical_not(there(0, ds)))
        def _():
            tile[16 * k:16 * k + 8, :] = jnp.zeros((8, 128), F32)
    tile[8:16, :] = mask_own[...]
    tile[24:32, :] = class_ref[...].astype(F32)
    tile[32:128, :] = jnp.zeros((96, 128), F32)
    strip[0:8, :] = jnp.zeros((8, 128), F32)
    strip[136:152, :] = jnp.zeros((16, 128), F32)
    strip[8:136, :] = tile[...].T
    near = strip[pl.ds(pl.multiple_of(16 * c, 16), 32), :]
    for j in range(16):
        mask[j] = jnp.broadcast_to(near[:, j + 4:j + 5], (32, 128))
    for j in range(8):
        kind = jnp.broadcast_to(near[8:24, 24 + j:25 + j], (16, 128))

        def fill(qg, _, j=j, kind=kind):
            value = jnp.zeros((16, 128), F32)
            for k in range(CLASSES):
                value = jnp.where(kind == float(k), gain_rows[qg, k:k + 1, :], value)
            gains[qg, 16 * j:16 * j + 16, :] = value
            return 0
        lax.fori_loop(0, 12, fill, 0)

    own_a.wait()
    for k in range(1, NSPEC):
        a_copy(k, incoming=True).wait_recv()
    for q in range(4):
        for g in range(3):
            pieces = []
            for rr in range(NSPEC):
                a, b = max(SLOT * rr, 128 * g) - SLOT * rr, min(SLOT * rr + SLOT, 128 * g + 128) - SLOT * rr
                if a >= b:
                    continue
                rel = q ^ (2 * (rr & 1))
                cut = min(b, KEPT[rel])
                if a < cut:
                    pieces.append(land_a[rr, BASE[rel] + a:BASE[rel] + cut, :])
                if cut < b:
                    pieces.append(jnp.zeros((b - max(a, cut), 128), F32))
            e0[3 * q + g, off_j(q):off_j(q) + 8, off_i(q):off_i(q) + 16, :] = (
                jnp.concatenate(pieces, axis=0).T.reshape(8, 16, 128))

    def heading(q):
        return (1 if LOWX[q] else -1), (1 if LOWY[q] else -1)

    def edge(q, kind):
        dx, dy = heading(q)
        return ((0, dy), (dx, 0), (dx, dy))[kind]

    def edge_copy(p, q, kind):
        dc, ds = edge(q, kind)
        groups = pl.ds(3 * q, 3)
        if kind == 0:
            src = e0.at[groups, pl.ds(8 if LOWY[q] else 0, 4), pl.ds(off_i(q), 16)]
            dst = yl.at[p, groups]
        elif kind == 1:
            src, dst = xs.at[groups], xl.at[p, groups]
        else:
            src, dst = cs.at[groups], cl.at[p, groups]
        return pltpu.make_async_remote_copy(
            src_ref=src, dst_ref=dst, send_sem=h_send.at[p, q, kind], recv_sem=h_recv.at[p, q, kind],
            device_id=at(dc, ds), device_id_type=MESH)

    def send_edges(p, q):
        i = 20 if LOWX[q] else 0
        jc = 8 if LOWY[q] else 0

        def pack(g, _):
            qg = 3 * q + g
            for j in range(8):
                xs[qg, j // 2, 4 * (j % 2):4 * (j % 2) + 4, :] = e0[qg, off_j(q) + j, i:i + 4, :]
            for j in range(4):
                cs[qg, j // 2, 4 * (j % 2):4 * (j % 2) + 4, :] = e0[qg, jc + j, i:i + 4, :]
            return 0
        lax.fori_loop(0, 3, pack, 0, unroll=3)
        for kind in range(3):
            @pl.when(there(*edge(q, kind)))
            def _():
                edge_copy(p, q, kind).start()

    def take_edges(p, q):
        i = 4 if LOWX[q] else 16
        jh = 0 if LOWY[q] else 8
        for kind in range(3):
            dc, ds = edge(q, kind)

            @pl.when(there(dc, ds))
            def _():
                edge_copy(p, q, kind).wait_send()

            @pl.when(there(-dc, -ds))
            def _():
                edge_copy(p, q, kind).wait_recv()

                def unpack(g, _):
                    qg = 3 * q + g
                    if kind == 0:
                        e0[qg, jh:jh + 4, off_i(q):off_i(q) + 16, :] = yl[p, qg]
                    else:
                        for j in range(8 if kind == 1 else 4):
                            got = (xl if kind == 1 else cl)[p, qg, j // 2, 4 * (j % 2):4 * (j % 2) + 4, :]
                            e0[qg, (off_j(q) if kind == 1 else jh) + j, i:i + 4, :] = got
                    return 0
                lax.fori_loop(0, 3, unpack, 0, unroll=3)

    def substep(q, t):
        src, dst = (e0, e1) if t % 2 == 0 else (e1, e0)
        if LOWY[q]:
            j0, n, dj, jm = t + 1, 11 - t, -1, 0
        else:
            j0, n, dj, jm = 0, 11 - t, 1, 4
        if LOWX[q]:
            di, im, starts = -1, 0, (8, 16) + (() if t == 3 else (1,))
        else:
            di, im, starts = 1, 8, (0, 8) + (() if t == 3 else (15,))

        def body(g, _):
            qg = 3 * q + g
            c0 = coef[0, pl.ds(qg, 1), :].reshape(1, 1, 128)
            cx = coef[1, pl.ds(qg, 1), :].reshape(1, 1, 128)
            cy = coef[2, pl.ds(qg, 1), :].reshape(1, 1, 128)
            for i in starts:
                mid = src[qg, j0:j0 + n, i:i + 8, :]
                along = src[qg, j0:j0 + n, i + di:i + di + 8, :]
                across = src[qg, j0 + dj:j0 + dj + n, i:i + 8, :]
                sea = mask[j0 + jm:j0 + jm + n, i + im:i + im + 8, :]
                dst[qg, j0:j0 + n, i:i + 8, :] = (c0 * mid + cx * along + cy * across) * sea
            return 0
        lax.fori_loop(0, 3, body, 0)

    def interior(q):
        return slice(off_j(q), off_j(q) + 8), slice(off_i(q), off_i(q) + 16)

    def place(qg):
        q = (qg >= 3).astype(I32) + (qg >= 6).astype(I32) + (qg >= 9).astype(I32)
        j = jnp.where(q < 2, 4, 0)
        i = pl.multiple_of(jnp.where(jnp.logical_or(q == 0, q == 3), 8, 0), 8)
        return pl.ds(j, 8), pl.ds(i, 16)

    def couple():
        for q in range(4):
            js, is_ = interior(q)
            for g in range(3):
                qg = 3 * q + g
                xb[:, 128 * qg:128 * qg + 128] = e0[qg, js, is_, :].reshape(128, 128).astype(BF16)

        def first(qg, _):
            got = jnp.dot(xb[...], weights[qg], preferred_element_type=F32)
            change = gains[qg] * got[:, :128] + got[:, 128:]
            slope[qg] = change
            js, is_ = place(qg)
            state = e0[qg, js, is_, :].reshape(128, 128)
            yb[:, pl.ds(pl.multiple_of(128 * qg, 128), 128)] = (state + change).astype(BF16)
            return 0
        lax.fori_loop(0, 12, first, 0, unroll=4)

        def second(qg, _):
            got = jnp.dot(yb[...], weights[qg], preferred_element_type=F32)
            change = gains[qg] * got[:, :128] + got[:, 128:]
            js, is_ = place(qg)
            state = e0[qg, js, is_, :].reshape(128, 128)
            e0[qg, js, is_, :] = (state + 0.5 * (slope[qg] + change)).reshape(8, 16, 128)
            return 0
        lax.fori_loop(0, 12, second, 0, unroll=4)

    def phase(p, _):
        for q in range(4):
            send_edges(p, q)
        for q in range(4):
            take_edges(p, q)

        @pl.when(jnp.logical_and(p > 0, p < PHASES - 1))
        def _():
            for q in range(4):
                substep(q, 0)
                substep(q, 1)
        for q in range(4):
            substep(q, 2)
            substep(q, 3)

        @pl.when(p < PHASES - 1)
        def _():
            couple()
        return 0

    lax.fori_loop(0, PHASES, phase, 0)

    for k in range(1, NSPEC):
        a_copy(k).wait_send()
    for q in range(4):
        js, is_ = interior(q)
        for g in range(3):
            block = e0[3 * q + g, js, is_, :].reshape(128, 128).T
            for rr in range(NSPEC):
                a, b = max(SLOT * rr, 128 * g), min(SLOT * rr + SLOT, 128 * g + 128)
                rel = q ^ (2 * (rr & 1))
                b = min(b, SLOT * rr + KEPT[rel])
                if a < b:
                    send_a[rr, BASE[rel] + a - SLOT * rr:BASE[rel] + b - SLOT * rr, :] = block[a - 128 * g:b - 128 * g]

    def b_copy(k, incoming=False):
        peer = lax.rem(r + k, NSPEC)
        slot = block_of(peer, half) if incoming else c
        return pltpu.make_async_remote_copy(
            src_ref=send_a.at[peer], dst_ref=land_b.at[slot], send_sem=b_send.at[k], recv_sem=b_recv.at[slot],
            device_id=(s, peer), device_id_type=MESH)

    for k in range(1, NSPEC):
        b_copy(k).start()
    own_b = pltpu.make_async_copy(send_a.at[r], land_b.at[c], b_send.at[0])
    own_b.start()
    own_b.wait()
    for k in range(1, NSPEC):
        b_copy(k, incoming=True).wait_recv()
    for rel in range(4):
        def unpack(f, _, rel=rel):
            rows = pl.ds(pl.multiple_of(BASE[rel] + 8 * f, 8), 8)
            parts = swap_blocks([land_b[cc, rows, :] for cc in range(8)])
            for j in range(8):
                out_ref[pl.ds((36 * f + 9 * rel) * 8 + j, 8, stride=8), :] = parts[j]
            return 0
        lax.fori_loop(0, FULL[rel], unpack, 0)
        n = FULL[rel]
        parts = swap_blocks([land_b[cc, BASE[rel] + 8 * n:BASE[rel] + 9 * n, :] for cc in range(8)])
        for j in range(8):
            out_ref[pl.ds((9 * rel + 8) * 8 + j, n, stride=288), :] = parts[j]
    for k in range(1, NSPEC):
        b_copy(k).wait_send()


def shards(ns, spectrum, ocean_mask, depth_class, freq_speed, coupling, source, gain_table):
    vmem, hbm = pl.BlockSpec(memory_space=pltpu.VMEM), pl.BlockSpec(memory_space=pl.ANY)
    dma = pltpu.SemaphoreType.DMA
    out = pl.pallas_call(
        functools.partial(kernel, ns),
        out_shape=jax.ShapeDtypeStruct((LOCAL * 8, 128), F32),
        in_specs=[vmem, vmem, vmem, pl.BlockSpec(memory_space=pltpu.SMEM), hbm, hbm, vmem],
        out_specs=vmem,
        scratch_shapes=[
            pltpu.VMEM((2, BINS, BINS), BF16),
            pltpu.VMEM((12, BINS, 256), BF16),
            pltpu.VMEM((12, 1536, 256), BF16),
            pltpu.VMEM((8, 256, 512), BF16),
            pltpu.VMEM((12, 12, 24, 128), F32),
            pltpu.VMEM((12, 12, 24, 128), F32),
            pltpu.VMEM((12, 128, 128), F32),
            pltpu.VMEM((128, 1536), BF16),
            pltpu.VMEM((128, 1536), BF16),
            pltpu.VMEM((12, 128, 128), F32),
            pltpu.VMEM((12, 8, 128), F32),
            pltpu.VMEM((16, 32, 128), F32),
            pltpu.VMEM((3, 16, 128), F32),
            pltpu.VMEM((8, ROWS, 128), F32),
            pltpu.VMEM((8, ROWS, 128), F32),
            pltpu.VMEM((8, ROWS, 128), F32),
            pltpu.VMEM((12, 4, 8, 128), F32),
            pltpu.VMEM((12, 2, 8, 128), F32),
            pltpu.VMEM((PHASES, 12, 4, 16, 128), F32),
            pltpu.VMEM((PHASES, 12, 4, 8, 128), F32),
            pltpu.VMEM((PHASES, 12, 2, 8, 128), F32),
            pltpu.VMEM((128, 128), F32),
            pltpu.VMEM((152, 128), F32),
            pltpu.VMEM((8, 128), F32),
            pltpu.VMEM((2, 8, 128), F32),
            dma((2,)), dma((8,)), dma((8,)), dma((8,)), dma((8,)),
            dma((PHASES, 4, 3)), dma((PHASES, 4, 3)), dma((2,)), dma((2,)),
        ],
        compiler_params=pltpu.CompilerParams(
            collective_id=0, has_side_effects=True, vmem_limit_bytes=56 * 2**20),
        cost_estimate=pl.CostEstimate(flops=12 * 10**9, bytes_accessed=9 * 10**6, transcendentals=0),
        name="wave_steps",
    )(spectrum.reshape(LOCAL * 8, 128), ocean_mask, depth_class, freq_speed, coupling, source, gain_table)
    return out.reshape(LOCAL, 8, 128)


def solution(mesh):
    placed = (P("spec", "space", None), P("space", None), P("space", None), P(), P(), P(), P())
    return jax.shard_map(
        functools.partial(shards, mesh.shape["space"]), mesh=mesh, in_specs=placed,
        out_specs=P("spec", "space", None), check_vma=False)
```

profile of v0, /device:TPU:16, one launch (start us, length us, event | category | flops | bytes accessed | tf_op | source)
XLA Modules:
  0.0 98.8 jit_solution(16454400218678019828)
XLA Ops:
  0.0 96.8 %wave_steps.1 = f32[1296,128]{1,0:T(8,128)} custom-call(f32[1296,128]{1,0:T(8,128)} %bitcast.3, s32[8,128]{1,0:T(8,128)} %mask_ref.1, s32[8,128]{1,0:T(8,128)} %class_ref.1, f32[36]{0:T(128)} %speed_ref.1, bf16[1296,1296]{1,0:T(8,128)(2,1)} %coupling_ref.1, bf16[1296,1296]{1,0:T(8,128)(2,1)} %source_ref.1, f32[8,1296]{1,0:T(8,128)} %gain_ref.1), custom_call_target="tpu_custom_call" | custom-call | flops 12000000000 | bytes 9000000 | tf_op jit(solution)/shard_map/wave_steps/pallas_call | solution.py:475
  96.8 2.0 %copy.9 = f32[162,8,128]{2,1,0:T(8,128)} copy(f32[162,8,128]{2,1,0:T(8,128)} %bitcast.2) | data formatting | bytes 1327104
where the time goes:
time: 99.6 us; the launch traced here: 98.8 us
  Pallas kernels  96.8 us (97%)
  local copies, waits for them, and re-layouts  1.97 us (2%)
    pallas_call x1, Pallas kernels, shards(): pl.pallas_call(functools.partial(kernel, ns), out_shape=jax.ShapeDtypeStr...  96.8 us

commit v1 on v0

--- a/solution.py
+++ b/solution.py
@@ -18,7 +18,8 @@
 BASE = (0, 48, 96, 136)
 KEPT = (48, 48, 40, 40)
 ROWS = 176
-LOWX, LOWY = (True, False, False, True), (True, True, False, False)
+QUADS = (0, 2, 1, 3)
+LOWX, LOWY = (True, False, False, True), (True, False, True, False)
 PAIRS = ((0, 0), (1, 0), (1, 1), (2, 1), (3, 1), (3, 2), (4, 2), (5, 2))
 PHASES = ITERS + 1
 
@@ -73,9 +74,13 @@
     return r, q ^ (2 * (r & 1)), slot - SLOT * r
 
 
+def relative(q, r):
+    return QUADS[q] ^ (2 * (r & 1))
+
+
 def kernel(ns, x_ref, mask_ref, class_ref, speed_ref, coupling_ref, source_ref, gain_ref, out_ref,
-           natural, turned, weights, pick, e0, e1, slope, xb, yb, gains, gain_rows, mask, coef,
-           send_a, land_a, land_b, xs, cs, yl, xl, cl, tile, strip, mask_own, mask_land,
+           natural, turned, weights, pick, e0, e1, slope, part, xb, yb, gains, gain_rows, mask, coef,
+           send_a, land_a, land_b, xs, cs, yl, xl, cl, tile, strip, kind, mask_own, mask_land,
            w_sem, a_send, a_recv, b_send, b_recv, h_send, h_recv, m_send, m_recv):
     r = lax.axis_index("spec")
     s = lax.axis_index("space")
@@ -107,17 +112,15 @@
     mask_own[...] = mask_ref[...].astype(F32)
 
     for rel in range(4):
-        def pack(f, _, rel=rel):
+        for f in range(FULL[rel]):
             parts = [x_ref[pl.ds((36 * f + 9 * rel) * 8 + j, 8, stride=8), :] for j in range(8)]
-            for cc, part in enumerate(swap_blocks(parts)):
-                send_a[cc, pl.ds(pl.multiple_of(BASE[rel] + 8 * f, 8), 8), :] = part
-            return 0
-        lax.fori_loop(0, FULL[rel], pack, 0)
+            for cc, block in enumerate(swap_blocks(parts)):
+                send_a[cc, BASE[rel] + 8 * f:BASE[rel] + 8 * f + 8, :] = block
         n = FULL[rel]
         parts = [x_ref[pl.ds((9 * rel + 8) * 8 + j, n, stride=288), :] for j in range(8)]
-        for cc, part in enumerate(swap_blocks(parts)):
+        for cc, block in enumerate(swap_blocks(parts)):
             send_a[cc, BASE[rel] + 8 * n:BASE[rel] + 8 * n + 8, :] = jnp.zeros((8, 128), F32)
-            send_a[cc, BASE[rel] + 8 * n:BASE[rel] + 9 * n, :] = part
+            send_a[cc, BASE[rel] + 8 * n:BASE[rel] + 9 * n, :] = block
 
     beside = (c > 0).astype(I32) + (c < NSPEC - 1).astype(I32)
     beyond = (s > 0).astype(I32) + (s < ns - 1).astype(I32)
@@ -154,7 +157,9 @@
 
     row = lax.broadcasted_iota(I32, (16, 128), 0)
     quad = (row >= 3).astype(I32) + (row >= 6).astype(I32) + (row >= 9).astype(I32)
-    home, rel, idx = places(quad, row - 3 * quad, (16, 128))
+    group = row - 3 * quad
+    quad = jnp.where(quad == 1, 2, jnp.where(quad == 2, 1, quad))
+    home, rel, idx = places(quad, group, (16, 128))
     here = local_bin(rel, idx)
     many = rel < 2
     whole = jnp.where(many, 40, 32)
@@ -179,7 +184,7 @@
     for k, (t, g) in enumerate(PAIRS):
         rows = 16 if t == 5 else 256
         for q in range(4):
-            home, rel, idx = places(jnp.full((1, 128), q, I32), g, (1, 128))
+            home, rel, idx = places(jnp.full((1, 128), QUADS[q], I32), g, (1, 128))
             want = LOCAL * home + local_bin(rel, idx) - 256 * t
             hit = lax.broadcasted_iota(I32, (rows, 128), 0) == want
             pick[k, 0:rows, 128 * q:128 * q + 128] = jnp.where(hit, 1.0, 0.0).astype(BF16)
@@ -201,8 +206,8 @@
     for g in range(3):
         total = to_quadrants(lambda at_, n: thirds[:, at_:at_ + n], g)
         for q in range(4):
-            part = total[:, 128 * q:128 * q + 128]
-            gain_rows[3 * q + g] = part[0:8] + part[8:16] + part[16:24]
+            third = total[:, 128 * q:128 * q + 128]
+            gain_rows[3 * q + g] = third[0:8] + third[8:16] + third[16:24]
 
     for copy in loads:
         copy.wait()
@@ -215,22 +220,6 @@
                     turned[3 * q + g, rows, 128 * m:128 * m + 128] = total[:, 128 * q:128 * q + 128]
             return 0
         lax.fori_loop(0, 9, columns, 0)
-
-    for rr in range(NSPEC):
-        blocks = []
-        for q in range(4):
-            place = lax.broadcasted_iota(I32, (SLOT, 176), 0)
-            want = local_bin(jnp.full((SLOT, 176), q ^ (2 * (rr & 1)), I32), place) + 2 * rr
-            hit = lax.broadcasted_iota(I32, (SLOT, 176), 1) == want
-            blocks.append(jnp.where(hit, 1.0, 0.0).astype(BF16))
-        onehot = jnp.concatenate(blocks, axis=0)
-
-        def lines(qg, _, rr=rr, onehot=onehot):
-            got = jnp.dot(onehot, turned[qg, 160 * rr:160 * rr + 176, :], preferred_element_type=F32).astype(BF16)
-            for q in range(4):
-                weights[qg, 384 * q + SLOT * rr:384 * q + SLOT * rr + SLOT, :] = got[SLOT * q:SLOT * q + SLOT]
-            return 0
-        lax.fori_loop(0, 12, lines, 0, unroll=2)
 
     for k, ds in ((0, -1), (1, 1)):
         @pl.when(there(0, ds))
@@ -252,34 +241,16 @@
     for j in range(16):
         mask[j] = jnp.broadcast_to(near[:, j + 4:j + 5], (32, 128))
     for j in range(8):
-        kind = jnp.broadcast_to(near[8:24, 24 + j:25 + j], (16, 128))
-
-        def fill(qg, _, j=j, kind=kind):
-            value = jnp.zeros((16, 128), F32)
-            for k in range(CLASSES):
-                value = jnp.where(kind == float(k), gain_rows[qg, k:k + 1, :], value)
-            gains[qg, 16 * j:16 * j + 16, :] = value
-            return 0
-        lax.fori_loop(0, 12, fill, 0)
-
-    own_a.wait()
-    for k in range(1, NSPEC):
-        a_copy(k, incoming=True).wait_recv()
-    for q in range(4):
-        for g in range(3):
-            pieces = []
-            for rr in range(NSPEC):
-                a, b = max(SLOT * rr, 128 * g) - SLOT * rr, min(SLOT * rr + SLOT, 128 * g + 128) - SLOT * rr
-                if a >= b:
-                    continue
-                rel = q ^ (2 * (rr & 1))
-                cut = min(b, KEPT[rel])
-                if a < cut:
-                    pieces.append(land_a[rr, BASE[rel] + a:BASE[rel] + cut, :])
-                if cut < b:
-                    pieces.append(jnp.zeros((b - max(a, cut), 128), F32))
-            e0[3 * q + g, off_j(q):off_j(q) + 8, off_i(q):off_i(q) + 16, :] = (
-                jnp.concatenate(pieces, axis=0).T.reshape(8, 16, 128))
+        kind[16 * j:16 * j + 16, :] = jnp.broadcast_to(near[8:24, 24 + j:25 + j], (16, 128))
+
+    def fill(qg, _):
+        which = kind[...]
+        value = jnp.zeros((128, 128), F32)
+        for k in range(CLASSES):
+            value = jnp.where(which == float(k), gain_rows[qg, k:k + 1, :], value)
+        gains[qg] = value
+        return 0
+    lax.fori_loop(0, 12, fill, 0)
 
     def heading(q):
         return (1 if LOWX[q] else -1), (1 if LOWY[q] else -1)
@@ -302,16 +273,21 @@
             src_ref=src, dst_ref=dst, send_sem=h_send.at[p, q, kind], recv_sem=h_recv.at[p, q, kind],
             device_id=at(dc, ds), device_id_type=MESH)
 
+    def corner(q, landed):
+        for d, (n, at_) in enumerate(((3, 0), (2, 3), (1, 5))):
+            j = (3 - d if landed else 11 - d) if LOWY[q] else (8 + d if landed else d)
+            i = ((8 if landed else 24) - n) if LOWX[q] else (16 if landed else 0)
+            yield n, at_, j, i
+
     def send_edges(p, q):
         i = 20 if LOWX[q] else 0
-        jc = 8 if LOWY[q] else 0
 
         def pack(g, _):
             qg = 3 * q + g
             for j in range(8):
                 xs[qg, j // 2, 4 * (j % 2):4 * (j % 2) + 4, :] = e0[qg, off_j(q) + j, i:i + 4, :]
-            for j in range(4):
-                cs[qg, j // 2, 4 * (j % 2):4 * (j % 2) + 4, :] = e0[qg, jc + j, i:i + 4, :]
+            for n, at_, j, ii in corner(q, False):
+                cs[qg, at_:at_ + n, :] = e0[qg, j, ii:ii + n, :]
             return 0
         lax.fori_loop(0, 3, pack, 0, unroll=3)
         for kind in range(3):
@@ -337,136 +313,193 @@
                     qg = 3 * q + g
                     if kind == 0:
                         e0[qg, jh:jh + 4, off_i(q):off_i(q) + 16, :] = yl[p, qg]
+                    elif kind == 1:
+                        for j in range(8):
+                            e0[qg, off_j(q) + j, i:i + 4, :] = xl[p, qg, j // 2, 4 * (j % 2):4 * (j % 2) + 4, :]
                     else:
-                        for j in range(8 if kind == 1 else 4):
-                            got = (xl if kind == 1 else cl)[p, qg, j // 2, 4 * (j % 2):4 * (j % 2) + 4, :]
-                            e0[qg, (off_j(q) if kind == 1 else jh) + j, i:i + 4, :] = got
+                        for n, at_, j, ii in corner(q, True):
+                            e0[qg, j, ii:ii + n, :] = cl[p, qg, at_:at_ + n, :]
                     return 0
                 lax.fori_loop(0, 3, unpack, 0, unroll=3)
 
     def substep(q, t):
         src, dst = (e0, e1) if t % 2 == 0 else (e1, e0)
         if LOWY[q]:
-            j0, n, dj, jm = t + 1, 11 - t, -1, 0
+            j0, n, jm = t + 1, 11 - t, 0
         else:
-            j0, n, dj, jm = 0, 11 - t, 1, 4
+            j0, n, jm = 0, 11 - t, 4
         if LOWX[q]:
             di, im, starts = -1, 0, (8, 16) + (() if t == 3 else (1,))
         else:
             di, im, starts = 1, 8, (0, 8) + (() if t == 3 else (15,))
 
+        groups = slice(3 * q, 3 * q + 3)
+        c0, cx, cy = (coef[k, groups, :].reshape(3, 1, 1, 128) for k in range(3))
+        for i in starts:
+            for first in range(j0, j0 + n, 4):
+                m = min(4, j0 + n - first)
+                if LOWY[q]:
+                    both = src[groups, first - 1:first + m, i:i + 8, :]
+                    mid, across = both[:, 1:], both[:, :-1]
+                else:
+                    both = src[groups, first:first + m + 1, i:i + 8, :]
+                    mid, across = both[:, :-1], both[:, 1:]
+                along = src[groups, first:first + m, i + di:i + di + 8, :]
+                sea = mask[first + jm:first + jm + m, i + im:i + im + 8, :][None]
+                dst[groups, first:first + m, i:i + 8, :] = (c0 * mid + cx * along + cy * across) * sea
+
+    def interior(q):
+        return slice(off_j(q), off_j(q) + 8), slice(off_i(q), off_i(q) + 16)
+
+    def place(qg):
+        q = (qg >= 3).astype(I32) + (qg >= 6).astype(I32) + (qg >= 9).astype(I32)
+        j = jnp.where(jnp.logical_or(q == 0, q == 2), 4, 0)
+        i = pl.multiple_of(jnp.where(jnp.logical_or(q == 0, q == 3), 8, 0), 8)
+        return pl.ds(j, 8), pl.ds(i, 16)
+
+    def narrow(q):
+        js, is_ = interior(q)
+        for g in range(3):
+            qg = 3 * q + g
+            xb[:, 128 * qg:128 * qg + 128] = e0[qg, js, is_, :].reshape(128, 128).astype(BF16)
+
+    def first_half(qg, _):
+        part[qg] = jnp.dot(xb[:, :768], weights[qg, :768, :], preferred_element_type=F32)
+        return 0
+
+    def second_half(qg, _):
+        got = part[qg] + jnp.dot(xb[:, 768:], weights[qg, 768:, :], preferred_element_type=F32)
+        change = gains[qg] * got[:, :128] + got[:, 128:]
+        slope[qg] = change
+        js, is_ = place(qg)
+        state = e0[qg, js, is_, :].reshape(128, 128)
+        yb[:, pl.ds(pl.multiple_of(128 * qg, 128), 128)] = (state + change).astype(BF16)
+        return 0
+
+    def finish(q):
+        js, is_ = interior(q)
+
         def body(g, _):
             qg = 3 * q + g
-            c0 = coef[0, pl.ds(qg, 1), :].reshape(1, 1, 128)
-            cx = coef[1, pl.ds(qg, 1), :].reshape(1, 1, 128)
-            cy = coef[2, pl.ds(qg, 1), :].reshape(1, 1, 128)
-            for i in starts:
-                mid = src[qg, j0:j0 + n, i:i + 8, :]
-                along = src[qg, j0:j0 + n, i + di:i + di + 8, :]
-                across = src[qg, j0 + dj:j0 + dj + n, i:i + 8, :]
-                sea = mask[j0 + jm:j0 + jm + n, i + im:i + im + 8, :]
-                dst[qg, j0:j0 + n, i:i + 8, :] = (c0 * mid + cx * along + cy * across) * sea
-            return 0
-        lax.fori_loop(0, 3, body, 0)
-
-    def interior(q):
-        return slice(off_j(q), off_j(q) + 8), slice(off_i(q), off_i(q) + 16)
-
-    def place(qg):
-        q = (qg >= 3).astype(I32) + (qg >= 6).astype(I32) + (qg >= 9).astype(I32)
-        j = jnp.where(q < 2, 4, 0)
-        i = pl.multiple_of(jnp.where(jnp.logical_or(q == 0, q == 3), 8, 0), 8)
-        return pl.ds(j, 8), pl.ds(i, 16)
-
-    def couple():
-        for q in range(4):
-            js, is_ = interior(q)
-            for g in range(3):
-                qg = 3 * q + g
-                xb[:, 128 * qg:128 * qg + 128] = e0[qg, js, is_, :].reshape(128, 128).astype(BF16)
-
-        def first(qg, _):
-            got = jnp.dot(xb[...], weights[qg], preferred_element_type=F32)
-            change = gains[qg] * got[:, :128] + got[:, 128:]
-            slope[qg] = change
-            js, is_ = place(qg)
-            state = e0[qg, js, is_, :].reshape(128, 128)
-            yb[:, pl.ds(pl.multiple_of(128 * qg, 128), 128)] = (state + change).astype(BF16)
-            return 0
-        lax.fori_loop(0, 12, first, 0, unroll=4)
-
-        def second(qg, _):
             got = jnp.dot(yb[...], weights[qg], preferred_element_type=F32)
             change = gains[qg] * got[:, :128] + got[:, 128:]
-            js, is_ = place(qg)
             state = e0[qg, js, is_, :].reshape(128, 128)
             e0[qg, js, is_, :] = (state + 0.5 * (slope[qg] + change)).reshape(8, 16, 128)
             return 0
-        lax.fori_loop(0, 12, second, 0, unroll=4)
+        lax.fori_loop(0, 3, body, 0, unroll=3)
+
+    own_a.wait()
+    for k in range(1, NSPEC):
+        a_copy(k, incoming=True).wait_recv()
+    for q in range(4):
+        for g in range(3):
+            pieces = []
+            for rr in range(NSPEC):
+                a, b = max(SLOT * rr, 128 * g) - SLOT * rr, min(SLOT * rr + SLOT, 128 * g + 128) - SLOT * rr
+                if a >= b:
+                    continue
+                rel = relative(q, rr)
+                cut = min(b, KEPT[rel])
+                if a < cut:
+                    pieces.append(land_a[rr, BASE[rel] + a:BASE[rel] + cut, :])
+                if cut < b:
+                    pieces.append(jnp.zeros((b - max(a, cut), 128), F32))
+            e0[3 * q + g, off_j(q):off_j(q) + 8, off_i(q):off_i(q) + 16, :] = (
+                jnp.concatenate(pieces, axis=0).T.reshape(8, 16, 128))
+        send_edges(0, q)
+
+    for rr in range(NSPEC):
+        blocks = []
+        for q in range(4):
+            spot = lax.broadcasted_iota(I32, (SLOT, 176), 0)
+            want = local_bin(jnp.full((SLOT, 176), relative(q, rr), I32), spot) + 2 * rr
+            hit = lax.broadcasted_iota(I32, (SLOT, 176), 1) == want
+            blocks.append(jnp.where(hit, 1.0, 0.0).astype(BF16))
+        onehot = jnp.concatenate(blocks, axis=0)
+
+        def lines(qg, _, rr=rr, onehot=onehot):
+            got = jnp.dot(onehot, turned[qg, 160 * rr:160 * rr + 176, :], preferred_element_type=F32).astype(BF16)
+            for q in range(4):
+                weights[qg, 384 * q + SLOT * rr:384 * q + SLOT * rr + SLOT, :] = got[SLOT * q:SLOT * q + SLOT]
+            return 0
+        lax.fori_loop(0, 12, lines, 0, unroll=2)
 
     def phase(p, _):
         for q in range(4):
-            send_edges(p, q)
-        for q in range(4):
             take_edges(p, q)
 
-        @pl.when(jnp.logical_and(p > 0, p < PHASES - 1))
-        def _():
-            for q in range(4):
+            @pl.when(p > 0)
+            def _():
                 substep(q, 0)
                 substep(q, 1)
-        for q in range(4):
             substep(q, 2)
             substep(q, 3)
-
-        @pl.when(p < PHASES - 1)
-        def _():
-            couple()
+            narrow(q)
+            if q == 1:
+                lax.fori_loop(0, 12, first_half, 0, unroll=4)
+        lax.fori_loop(0, 12, second_half, 0, unroll=4)
+        for q in range(4):
+            finish(q)
+            send_edges(p + 1, q)
         return 0
 
-    lax.fori_loop(0, PHASES, phase, 0)
+    lax.fori_loop(0, ITERS, phase, 0)
 
     for k in range(1, NSPEC):
         a_copy(k).wait_send()
+
+    def b_copy(k, q, odd, incoming=False):
+        peer = lax.rem(r + k, NSPEC)
+        slot = block_of(peer, half) if incoming else c
+        rel = relative(q, odd)
+        rows = pl.ds(BASE[rel], KEPT[rel])
+        return pltpu.make_async_remote_copy(
+            src_ref=send_a.at[peer, rows], dst_ref=land_b.at[slot, rows],
+            send_sem=b_send.at[k, q], recv_sem=b_recv.at[slot, rel], device_id=(s, peer), device_id_type=MESH)
+
     for q in range(4):
+        take_edges(ITERS, q)
+        substep(q, 2)
+        substep(q, 3)
         js, is_ = interior(q)
         for g in range(3):
             block = e0[3 * q + g, js, is_, :].reshape(128, 128).T
             for rr in range(NSPEC):
                 a, b = max(SLOT * rr, 128 * g), min(SLOT * rr + SLOT, 128 * g + 128)
-                rel = q ^ (2 * (rr & 1))
+                rel = relative(q, rr)
                 b = min(b, SLOT * rr + KEPT[rel])
                 if a < b:
                     send_a[rr, BASE[rel] + a - SLOT * rr:BASE[rel] + b - SLOT * rr, :] = block[a - 128 * g:b - 128 * g]
-
-    def b_copy(k, incoming=False):
-        peer = lax.rem(r + k, NSPEC)
-        slot = block_of(peer, half) if incoming else c
-        return pltpu.make_async_remote_copy(
-            src_ref=send_a.at[peer], dst_ref=land_b.at[slot], send_sem=b_send.at[k], recv_sem=b_recv.at[slot],
-            device_id=(s, peer), device_id_type=MESH)
-
-    for k in range(1, NSPEC):
-        b_copy(k).start()
-    own_b = pltpu.make_async_copy(send_a.at[r], land_b.at[c], b_send.at[0])
+        for k in range(1, NSPEC):
+            for odd in range(2):
+                @pl.when(lax.rem(r + k, 2) == odd)
+                def _():
+                    b_copy(k, q, odd).start()
+    own_b = pltpu.make_async_copy(send_a.at[r], land_b.at[c], a_send.at[0])
     own_b.start()
     own_b.wait()
     for k in range(1, NSPEC):
-        b_copy(k, incoming=True).wait_recv()
+        for q in range(4):
+            for odd in range(2):
+                @pl.when(lax.rem(r, 2) == odd)
+                def _():
+                    b_copy(k, q, odd, incoming=True).wait_recv()
     for rel in range(4):
-        def unpack(f, _, rel=rel):
-            rows = pl.ds(pl.multiple_of(BASE[rel] + 8 * f, 8), 8)
+        for f in range(FULL[rel]):
+            rows = slice(BASE[rel] + 8 * f, BASE[rel] + 8 * f + 8)
             parts = swap_blocks([land_b[cc, rows, :] for cc in range(8)])
             for j in range(8):
                 out_ref[pl.ds((36 * f + 9 * rel) * 8 + j, 8, stride=8), :] = parts[j]
-            return 0
-        lax.fori_loop(0, FULL[rel], unpack, 0)
         n = FULL[rel]
         parts = swap_blocks([land_b[cc, BASE[rel] + 8 * n:BASE[rel] + 9 * n, :] for cc in range(8)])
         for j in range(8):
             out_ref[pl.ds((9 * rel + 8) * 8 + j, n, stride=288), :] = parts[j]
     for k in range(1, NSPEC):
-        b_copy(k).wait_send()
+        for q in range(4):
+            for odd in range(2):
+                @pl.when(lax.rem(r + k, 2) == odd)
+                def _():
+                    b_copy(k, q, odd).wait_send()
 
 
 def shards(ns, spectrum, ocean_mask, depth_class, freq_speed, coupling, source, gain_table):
@@ -485,6 +518,7 @@
             pltpu.VMEM((12, 12, 24, 128), F32),
             pltpu.VMEM((12, 12, 24, 128), F32),
             pltpu.VMEM((12, 128, 128), F32),
+            pltpu.VMEM((12, 128, 256), F32),
             pltpu.VMEM((128, 1536), BF16),
             pltpu.VMEM((128, 1536), BF16),
             pltpu.VMEM((12, 128, 128), F32),
@@ -495,15 +529,16 @@
             pltpu.VMEM((8, ROWS, 128), F32),
             pltpu.VMEM((8, ROWS, 128), F32),
             pltpu.VMEM((12, 4, 8, 128), F32),
-            pltpu.VMEM((12, 2, 8, 128), F32),
+            pltpu.VMEM((12, 8, 128), F32),
             pltpu.VMEM((PHASES, 12, 4, 16, 128), F32),
             pltpu.VMEM((PHASES, 12, 4, 8, 128), F32),
-            pltpu.VMEM((PHASES, 12, 2, 8, 128), F32),
+            pltpu.VMEM((PHASES, 12, 8, 128), F32),
             pltpu.VMEM((128, 128), F32),
             pltpu.VMEM((152, 128), F32),
+            pltpu.VMEM((128, 128), F32),
             pltpu.VMEM((8, 128), F32),
             pltpu.VMEM((2, 8, 128), F32),
-            dma((2,)), dma((8,)), dma((8,)), dma((8,)), dma((8,)),
+            dma((2,)), dma((8,)), dma((8,)), dma((8, 4)), dma((8, 4)),
             dma((PHASES, 4, 3)), dma((PHASES, 4, 3)), dma((2,)), dma((2,)),
         ],
         compiler_params=pltpu.CompilerParams(

time: 99.6 us -> 80.8 us (0.81)
  Pallas kernels: 96.8 us -> 78.6 us
    pallas_call x1, Pallas kernels: 96.8 us -> 78.6 us  [shards(): pl.pallas_call(functools.partial(kernel, ns), out_shape=jax.ShapeDtypeStr...]
where the time goes in v1:
time: 80.8 us; the launch traced here: 80.6 us
  Pallas kernels  78.6 us (97%)
  local copies, waits for them, and re-layouts  1.97 us (2%)
    pallas_call x1, Pallas kernels, shards(): pl.pallas_call(functools.partial(kernel, ns), out_shape=jax.ShapeDtypeStr...  78.6 us
    unnamed x1, local copies, waits for them, and re-layouts  1.97 us

profile of v1, /device:TPU:16, one launch (start us, length us, event | category | flops | bytes accessed | tf_op | source)
XLA Modules:
  0.0 80.6 jit_solution(11431975713197228049)
XLA Ops:
  0.0 78.6 %wave_steps.1 = f32[1296,128]{1,0:T(8,128)} custom-call(f32[1296,128]{1,0:T(8,128)} %bitcast.3, s32[8,128]{1,0:T(8,128)} %mask_ref.1, s32[8,128]{1,0:T(8,128)} %class_ref.1, f32[36]{0:T(128)} %speed_ref.1, bf16[1296,1296]{1,0:T(8,128)(2,1)} %coupling_ref.1, bf16[1296,1296]{1,0:T(8,128)(2,1)} %source_ref.1, f32[8,1296]{1,0:T(8,128)} %gain_ref.1), custom_call_target="tpu_custom_call" | custom-call | flops 12000000000 | bytes 9000000 | tf_op jit(solution)/shard_map/wave_steps/pallas_call | solution.py:508
  78.6 2.0 %copy.9 = f32[162,8,128]{2,1,0:T(8,128)} copy(f32[162,8,128]{2,1,0:T(8,128)} %bitcast.2) | data formatting | bytes 1327104

commit v2 on v1

--- a/solution.py
+++ b/solution.py
@@ -17,6 +17,7 @@
 FULL = (5, 5, 4, 4)
 BASE = (0, 48, 96, 136)
 KEPT = (48, 48, 40, 40)
+LIVE = (45, 45, 36, 36)
 ROWS = 176
 QUADS = (0, 2, 1, 3)
 LOWX, LOWY = (True, False, False, True), (True, False, True, False)
@@ -79,9 +80,9 @@
 
 
 def kernel(ns, x_ref, mask_ref, class_ref, speed_ref, coupling_ref, source_ref, gain_ref, out_ref,
-           natural, turned, weights, pick, e0, e1, slope, part, xb, yb, gains, gain_rows, mask, coef,
+           natural, turned, weights, pick, lift, e0, e1, slope, part, xb, yb, gains, gain_rows, mask, coef,
            send_a, land_a, land_b, xs, cs, yl, xl, cl, tile, strip, kind, mask_own, mask_land,
-           w_sem, a_send, a_recv, b_send, b_recv, h_send, h_recv, m_send, m_recv):
+           w_sem, a_send, a_recv, b_send, b_recv, own_sem, h_send, h_recv, m_send, m_recv):
     r = lax.axis_index("spec")
     s = lax.axis_index("space")
     half = s // (ns // 2)
@@ -100,6 +101,10 @@
     loads = [pltpu.make_async_copy(ref, natural.at[m], w_sem.at[m]) for m, ref in enumerate((coupling_ref, source_ref))]
     for copy in loads:
         copy.start()
+    for slot in range(NSPEC):
+        for rel in range(4):
+            end = BASE[rel] + KEPT[rel]
+            land_a[slot, end - 8:end, :] = jnp.zeros((8, 128), F32)
     barrier = pltpu.get_barrier_semaphore()
     around = [(dc, ds) for ds in (-1, 1) for dc in (-1, 0, 1)]
     for k in range(1, NSPEC):
@@ -126,16 +131,18 @@
     beyond = (s > 0).astype(I32) + (s < ns - 1).astype(I32)
     pl.semaphore_wait(barrier, NSPEC - 1 + beyond * (1 + beside))
 
-    def a_copy(k, incoming=False):
+    def a_copy(k, rel, incoming=False):
         peer = lax.rem(r + k, NSPEC)
+        slot = peer if incoming else r
+        rows = pl.ds(BASE[rel], LIVE[rel])
         return pltpu.make_async_remote_copy(
-            src_ref=send_a.at[block_of(peer, half)], dst_ref=land_a.at[peer if incoming else r],
-            send_sem=a_send.at[k], recv_sem=a_recv.at[peer if incoming else r],
-            device_id=(s, peer), device_id_type=MESH)
-
-    for k in range(1, NSPEC):
-        a_copy(k).start()
-    own_a = pltpu.make_async_copy(send_a.at[c], land_a.at[r], a_send.at[0])
+            src_ref=send_a.at[block_of(peer, half), rows], dst_ref=land_a.at[slot, rows],
+            send_sem=a_send.at[k, rel], recv_sem=a_recv.at[slot, rel], device_id=(s, peer), device_id_type=MESH)
+
+    for rel in range(4):
+        for k in range(1, NSPEC):
+            a_copy(k, rel).start()
+    own_a = pltpu.make_async_copy(send_a.at[c], land_a.at[r], own_sem)
     own_a.start()
 
     def mask_copy(ds, incoming=False):
@@ -187,16 +194,18 @@
             home, rel, idx = places(jnp.full((1, 128), QUADS[q], I32), g, (1, 128))
             want = LOCAL * home + local_bin(rel, idx) - 256 * t
             hit = lax.broadcasted_iota(I32, (rows, 128), 0) == want
-            pick[k, 0:rows, 128 * q:128 * q + 128] = jnp.where(hit, 1.0, 0.0).astype(BF16)
+            pick[256 * k:256 * k + rows, 128 * q:128 * q + 128] = jnp.where(hit, 1.0, 0.0).astype(BF16)
 
     def to_quadrants(lhs, g):
-        total = None
-        for k, (t, gg) in enumerate(PAIRS):
-            if gg == g:
-                rows = 16 if t == 5 else 256
-                term = jnp.dot(lhs(256 * t, rows), pick[k, 0:rows, :], preferred_element_type=F32)
-                total = term if total is None else total + term
-        return total
+        first, start, depth = ((0, 0, 512), (2, 256, 768), (5, 768, 528))[g]
+        return jnp.dot(lhs(start, depth), pick[256 * first:256 * first + depth, :], preferred_element_type=F32)
+
+    for rr in range(NSPEC):
+        for q in range(4):
+            spot = lax.broadcasted_iota(I32, (SLOT, 176), 0)
+            want = local_bin(jnp.full((SLOT, 176), relative(q, rr), I32), spot) + 2 * rr
+            hit = lax.broadcasted_iota(I32, (SLOT, 176), 1) == want
+            lift[rr, SLOT * q:SLOT * q + SLOT, :] = jnp.where(hit, 1.0, 0.0).astype(BF16)
 
     table = gain_ref[...]
     high = table.astype(BF16).astype(F32)
@@ -213,13 +222,13 @@
         copy.wait()
     for m in range(2):
         def columns(k, _, m=m):
-            rows = pl.ds(pl.multiple_of(144 * k, 16), 144)
+            rows = pl.ds(pl.multiple_of(432 * k, 16), 432)
             for g in range(3):
                 total = to_quadrants(lambda at_, n: natural[m, rows, at_:at_ + n], g).astype(BF16)
                 for q in range(4):
                     turned[3 * q + g, rows, 128 * m:128 * m + 128] = total[:, 128 * q:128 * q + 128]
             return 0
-        lax.fori_loop(0, 9, columns, 0)
+        lax.fori_loop(0, 3, columns, 0)
 
     for k, ds in ((0, -1), (1, 1)):
         @pl.when(there(0, ds))
@@ -351,46 +360,36 @@
     def interior(q):
         return slice(off_j(q), off_j(q) + 8), slice(off_i(q), off_i(q) + 16)
 
-    def place(qg):
-        q = (qg >= 3).astype(I32) + (qg >= 6).astype(I32) + (qg >= 9).astype(I32)
-        j = jnp.where(jnp.logical_or(q == 0, q == 2), 4, 0)
-        i = pl.multiple_of(jnp.where(jnp.logical_or(q == 0, q == 3), 8, 0), 8)
-        return pl.ds(j, 8), pl.ds(i, 16)
-
     def narrow(q):
         js, is_ = interior(q)
         for g in range(3):
             qg = 3 * q + g
             xb[:, 128 * qg:128 * qg + 128] = e0[qg, js, is_, :].reshape(128, 128).astype(BF16)
 
-    def first_half(qg, _):
+    def first_half(qg):
         part[qg] = jnp.dot(xb[:, :768], weights[qg, :768, :], preferred_element_type=F32)
-        return 0
-
-    def second_half(qg, _):
+
+    def second_half(qg):
         got = part[qg] + jnp.dot(xb[:, 768:], weights[qg, 768:, :], preferred_element_type=F32)
         change = gains[qg] * got[:, :128] + got[:, 128:]
         slope[qg] = change
-        js, is_ = place(qg)
+        js, is_ = interior(qg // 3)
         state = e0[qg, js, is_, :].reshape(128, 128)
-        yb[:, pl.ds(pl.multiple_of(128 * qg, 128), 128)] = (state + change).astype(BF16)
-        return 0
+        yb[:, 128 * qg:128 * qg + 128] = (state + change).astype(BF16)
 
     def finish(q):
         js, is_ = interior(q)
 
-        def body(g, _):
-            qg = 3 * q + g
+        for qg in range(3 * q, 3 * q + 3):
             got = jnp.dot(yb[...], weights[qg], preferred_element_type=F32)
             change = gains[qg] * got[:, :128] + got[:, 128:]
             state = e0[qg, js, is_, :].reshape(128, 128)
             e0[qg, js, is_, :] = (state + 0.5 * (slope[qg] + change)).reshape(8, 16, 128)
-            return 0
-        lax.fori_loop(0, 3, body, 0, unroll=3)
 
     own_a.wait()
-    for k in range(1, NSPEC):
-        a_copy(k, incoming=True).wait_recv()
+    for rel in range(4):
+        for k in range(1, NSPEC):
+            a_copy(k, rel, incoming=True).wait_recv()
     for q in range(4):
         for g in range(3):
             pieces = []
@@ -408,21 +407,13 @@
                 jnp.concatenate(pieces, axis=0).T.reshape(8, 16, 128))
         send_edges(0, q)
 
-    for rr in range(NSPEC):
-        blocks = []
-        for q in range(4):
-            spot = lax.broadcasted_iota(I32, (SLOT, 176), 0)
-            want = local_bin(jnp.full((SLOT, 176), relative(q, rr), I32), spot) + 2 * rr
-            hit = lax.broadcasted_iota(I32, (SLOT, 176), 1) == want
-            blocks.append(jnp.where(hit, 1.0, 0.0).astype(BF16))
-        onehot = jnp.concatenate(blocks, axis=0)
-
-        def lines(qg, _, rr=rr, onehot=onehot):
-            got = jnp.dot(onehot, turned[qg, 160 * rr:160 * rr + 176, :], preferred_element_type=F32).astype(BF16)
+    def lines(qg, _):
+        for rr in range(NSPEC):
+            got = jnp.dot(lift[rr], turned[qg, 160 * rr:160 * rr + 176, :], preferred_element_type=F32).astype(BF16)
             for q in range(4):
                 weights[qg, 384 * q + SLOT * rr:384 * q + SLOT * rr + SLOT, :] = got[SLOT * q:SLOT * q + SLOT]
-            return 0
-        lax.fori_loop(0, 12, lines, 0, unroll=2)
+        return 0
+    lax.fori_loop(0, 12, lines, 0)
 
     def phase(p, _):
         for q in range(4):
@@ -436,8 +427,10 @@
             substep(q, 3)
             narrow(q)
             if q == 1:
-                lax.fori_loop(0, 12, first_half, 0, unroll=4)
-        lax.fori_loop(0, 12, second_half, 0, unroll=4)
+                for qg in range(12):
+                    first_half(qg)
+        for qg in range(12):
+            second_half(qg)
         for q in range(4):
             finish(q)
             send_edges(p + 1, q)
@@ -445,14 +438,15 @@
 
     lax.fori_loop(0, ITERS, phase, 0)
 
-    for k in range(1, NSPEC):
-        a_copy(k).wait_send()
+    for rel in range(4):
+        for k in range(1, NSPEC):
+            a_copy(k, rel).wait_send()
 
     def b_copy(k, q, odd, incoming=False):
         peer = lax.rem(r + k, NSPEC)
         slot = block_of(peer, half) if incoming else c
         rel = relative(q, odd)
-        rows = pl.ds(BASE[rel], KEPT[rel])
+        rows = pl.ds(BASE[rel], LIVE[rel])
         return pltpu.make_async_remote_copy(
             src_ref=send_a.at[peer, rows], dst_ref=land_b.at[slot, rows],
             send_sem=b_send.at[k, q], recv_sem=b_recv.at[slot, rel], device_id=(s, peer), device_id_type=MESH)
@@ -475,25 +469,28 @@
                 @pl.when(lax.rem(r + k, 2) == odd)
                 def _():
                     b_copy(k, q, odd).start()
-    own_b = pltpu.make_async_copy(send_a.at[r], land_b.at[c], a_send.at[0])
+    own_b = pltpu.make_async_copy(send_a.at[r], land_b.at[c], own_sem)
     own_b.start()
-    own_b.wait()
-    for k in range(1, NSPEC):
-        for q in range(4):
-            for odd in range(2):
-                @pl.when(lax.rem(r, 2) == odd)
-                def _():
-                    b_copy(k, q, odd, incoming=True).wait_recv()
-    for rel in range(4):
-        for f in range(FULL[rel]):
+
+    def put(rel):
+        n = FULL[rel]
+        for f in range(n):
             rows = slice(BASE[rel] + 8 * f, BASE[rel] + 8 * f + 8)
             parts = swap_blocks([land_b[cc, rows, :] for cc in range(8)])
             for j in range(8):
                 out_ref[pl.ds((36 * f + 9 * rel) * 8 + j, 8, stride=8), :] = parts[j]
-        n = FULL[rel]
         parts = swap_blocks([land_b[cc, BASE[rel] + 8 * n:BASE[rel] + 9 * n, :] for cc in range(8)])
         for j in range(8):
             out_ref[pl.ds((9 * rel + 8) * 8 + j, n, stride=288), :] = parts[j]
+
+    own_b.wait()
+    for odd in range(2):
+        @pl.when(lax.rem(r, 2) == odd)
+        def _():
+            for q in range(4):
+                for k in range(1, NSPEC):
+                    b_copy(k, q, odd, incoming=True).wait_recv()
+                put(relative(q, odd))
     for k in range(1, NSPEC):
         for q in range(4):
             for odd in range(2):
@@ -514,7 +511,8 @@
             pltpu.VMEM((2, BINS, BINS), BF16),
             pltpu.VMEM((12, BINS, 256), BF16),
             pltpu.VMEM((12, 1536, 256), BF16),
-            pltpu.VMEM((8, 256, 512), BF16),
+            pltpu.VMEM((2048, 512), BF16),
+            pltpu.VMEM((NSPEC, 192, 176), BF16),
             pltpu.VMEM((12, 12, 24, 128), F32),
             pltpu.VMEM((12, 12, 24, 128), F32),
             pltpu.VMEM((12, 128, 128), F32),
@@ -538,7 +536,7 @@
             pltpu.VMEM((128, 128), F32),
             pltpu.VMEM((8, 128), F32),
             pltpu.VMEM((2, 8, 128), F32),
-            dma((2,)), dma((8,)), dma((8,)), dma((8, 4)), dma((8, 4)),
+            dma((2,)), dma((8, 4)), dma((8, 4)), dma((8, 4)), dma((8, 4)), dma,
             dma((PHASES, 4, 3)), dma((PHASES, 4, 3)), dma((2,)), dma((2,)),
         ],
         compiler_params=pltpu.CompilerParams(

time: 80.8 us -> 68.6 us (0.85)
  Pallas kernels: 78.6 us -> 66.4 us
    pallas_call x1, Pallas kernels: 78.6 us -> 66.4 us  [shards(): pl.pallas_call(functools.partial(kernel, ns), out_shape=jax.ShapeDtypeStr...]
where the time goes in v2:
time: 68.6 us; the launch traced here: 68.4 us
  Pallas kernels  66.4 us (97%)
  local copies, waits for them, and re-layouts  1.97 us (3%)
    pallas_call x1, Pallas kernels, shards(): pl.pallas_call(functools.partial(kernel, ns), out_shape=jax.ShapeDtypeStr...  66.4 us
    unnamed x1, local copies, waits for them, and re-layouts  1.97 us

profile of v2, /device:TPU:16, one launch (start us, length us, event | category | flops | bytes accessed | tf_op | source)
XLA Modules:
  0.0 68.4 jit_solution(11432923246174570975)
XLA Ops:
  0.0 66.4 %wave_steps.1 = f32[1296,128]{1,0:T(8,128)} custom-call(f32[1296,128]{1,0:T(8,128)} %bitcast.3, s32[8,128]{1,0:T(8,128)} %mask_ref.1, s32[8,128]{1,0:T(8,128)} %class_ref.1, f32[36]{0:T(128)} %speed_ref.1, bf16[1296,1296]{1,0:T(8,128)(2,1)} %coupling_ref.1, bf16[1296,1296]{1,0:T(8,128)(2,1)} %source_ref.1, f32[8,1296]{1,0:T(8,128)} %gain_ref.1), custom_call_target="tpu_custom_call" | custom-call | flops 12000000000 | bytes 9000000 | tf_op jit(solution)/shard_map/wave_steps/pallas_call | solution.py:505
  66.4 2.0 %copy.9 = f32[162,8,128]{2,1,0:T(8,128)} copy(f32[162,8,128]{2,1,0:T(8,128)} %bitcast.2) | data formatting | bytes 1327104

commit v3 on v2

--- a/solution.py
+++ b/solution.py
@@ -79,10 +79,10 @@
     return QUADS[q] ^ (2 * (r & 1))
 
 
-def kernel(ns, x_ref, mask_ref, class_ref, speed_ref, coupling_ref, source_ref, gain_ref, out_ref,
-           natural, turned, weights, pick, lift, e0, e1, slope, part, xb, yb, gains, gain_rows, mask, coef,
-           send_a, land_a, land_b, xs, cs, yl, xl, cl, tile, strip, kind, mask_own, mask_land,
-           w_sem, a_send, a_recv, b_send, b_recv, own_sem, h_send, h_recv, m_send, m_recv):
+def kernel(ns, spectrum_ref, mask_ref, class_ref, speed_ref, coupling_ref, source_ref, gain_ref, result_ref,
+           x_ref, out_ref, natural, turned, weights, pick, lift, e0, e1, slope, part, xb, yb, gains, gain_rows, mask, coef,
+           send_a, land_a, land_b, ys, xs, cs, yl, xl, cl, tile, strip, kind, mask_own, mask_land,
+           w_sem, a_send, a_recv, b_send, b_recv, own_sem, x_sem, o_sem, h_send, h_recv, m_send, m_recv):
     r = lax.axis_index("spec")
     s = lax.axis_index("space")
     half = s // (ns // 2)
@@ -98,9 +98,9 @@
             ok = cond if ok is None else jnp.logical_and(ok, cond)
         return ok
 
+    take_x = pltpu.make_async_copy(spectrum_ref, x_ref, x_sem)
+    take_x.start()
     loads = [pltpu.make_async_copy(ref, natural.at[m], w_sem.at[m]) for m, ref in enumerate((coupling_ref, source_ref))]
-    for copy in loads:
-        copy.start()
     for slot in range(NSPEC):
         for rel in range(4):
             end = BASE[rel] + KEPT[rel]
@@ -114,7 +114,16 @@
         def _():
             pl.semaphore_signal(barrier, inc=1, device_id=at(dc, ds), device_id_type=MESH)
 
+    for copy in loads:
+        copy.start()
     mask_own[...] = mask_ref[...].astype(F32)
+
+    def clear(qg, _):
+        e0[qg] = jnp.zeros((12, 24, 128), F32)
+        e1[qg] = jnp.zeros((12, 24, 128), F32)
+        return 0
+    lax.fori_loop(0, 12, clear, 0)
+    take_x.wait()
 
     for rel in range(4):
         for f in range(FULL[rel]):
@@ -155,12 +164,6 @@
         @pl.when(there(0, ds))
         def _():
             mask_copy(ds).start()
-
-    def clear(qg, _):
-        e0[qg] = jnp.zeros((12, 24, 128), F32)
-        e1[qg] = jnp.zeros((12, 24, 128), F32)
-        return 0
-    lax.fori_loop(0, 12, clear, 0)
 
     row = lax.broadcasted_iota(I32, (16, 128), 0)
     quad = (row >= 3).astype(I32) + (row >= 6).astype(I32) + (row >= 9).astype(I32)
@@ -271,16 +274,10 @@
     def edge_copy(p, q, kind):
         dc, ds = edge(q, kind)
         groups = pl.ds(3 * q, 3)
-        if kind == 0:
-            src = e0.at[groups, pl.ds(8 if LOWY[q] else 0, 4), pl.ds(off_i(q), 16)]
-            dst = yl.at[p, groups]
-        elif kind == 1:
-            src, dst = xs.at[groups], xl.at[p, groups]
-        else:
-            src, dst = cs.at[groups], cl.at[p, groups]
+        src, dst = ((ys, yl), (xs, xl), (cs, cl))[kind]
         return pltpu.make_async_remote_copy(
-            src_ref=src, dst_ref=dst, send_sem=h_send.at[p, q, kind], recv_sem=h_recv.at[p, q, kind],
-            device_id=at(dc, ds), device_id_type=MESH)
+            src_ref=src.at[groups], dst_ref=dst.at[p, groups], send_sem=h_send.at[p, q, kind],
+            recv_sem=h_recv.at[p, q, kind], device_id=at(dc, ds), device_id_type=MESH)
 
     def corner(q, landed):
         for d, (n, at_) in enumerate(((3, 0), (2, 3), (1, 5))):
@@ -290,36 +287,37 @@
 
     def send_edges(p, q):
         i = 20 if LOWX[q] else 0
-
-        def pack(g, _):
-            qg = 3 * q + g
-            for j in range(8):
-                xs[qg, j // 2, 4 * (j % 2):4 * (j % 2) + 4, :] = e0[qg, off_j(q) + j, i:i + 4, :]
-            for n, at_, j, ii in corner(q, False):
-                cs[qg, at_:at_ + n, :] = e0[qg, j, ii:ii + n, :]
-            return 0
-        lax.fori_loop(0, 3, pack, 0, unroll=3)
-        for kind in range(3):
+        jy = 8 if LOWY[q] else 0
+        groups = range(3 * q, 3 * q + 3)
+
+        def start(kind):
             @pl.when(there(*edge(q, kind)))
             def _():
                 edge_copy(p, q, kind).start()
 
+        for qg in groups:
+            for n, at_, j, ii in corner(q, False):
+                cs[qg, at_:at_ + n, :] = e0[qg, j, ii:ii + n, :]
+        start(2)
+        for qg in groups:
+            ys[qg] = e0[qg, jy:jy + 4, off_i(q):off_i(q) + 16, :]
+        start(0)
+        for qg in groups:
+            for j in range(8):
+                xs[qg, j // 2, 4 * (j % 2):4 * (j % 2) + 4, :] = e0[qg, off_j(q) + j, i:i + 4, :]
+        start(1)
+
     def take_edges(p, q):
         i = 4 if LOWX[q] else 16
         jh = 0 if LOWY[q] else 8
+        groups = range(3 * q, 3 * q + 3)
         for kind in range(3):
             dc, ds = edge(q, kind)
-
-            @pl.when(there(dc, ds))
-            def _():
-                edge_copy(p, q, kind).wait_send()
 
             @pl.when(there(-dc, -ds))
             def _():
                 edge_copy(p, q, kind).wait_recv()
-
-                def unpack(g, _):
-                    qg = 3 * q + g
+                for qg in groups:
                     if kind == 0:
                         e0[qg, jh:jh + 4, off_i(q):off_i(q) + 16, :] = yl[p, qg]
                     elif kind == 1:
@@ -328,8 +326,13 @@
                     else:
                         for n, at_, j, ii in corner(q, True):
                             e0[qg, j, ii:ii + n, :] = cl[p, qg, at_:at_ + n, :]
-                    return 0
-                lax.fori_loop(0, 3, unpack, 0, unroll=3)
+
+    def settle_edges(p):
+        for q in range(4):
+            for kind in range(3):
+                @pl.when(there(*edge(q, kind)))
+                def _():
+                    edge_copy(p, q, kind).wait_send()
 
     def substep(q, t):
         src, dst = (e0, e1) if t % 2 == 0 else (e1, e0)
@@ -431,6 +434,7 @@
                     first_half(qg)
         for qg in range(12):
             second_half(qg)
+        settle_edges(p)
         for q in range(4):
             finish(q)
             send_edges(p + 1, q)
@@ -469,6 +473,7 @@
                 @pl.when(lax.rem(r + k, 2) == odd)
                 def _():
                     b_copy(k, q, odd).start()
+    settle_edges(ITERS)
     own_b = pltpu.make_async_copy(send_a.at[r], land_b.at[c], own_sem)
     own_b.start()
 
@@ -482,6 +487,12 @@
         parts = swap_blocks([land_b[cc, BASE[rel] + 8 * n:BASE[rel] + 9 * n, :] for cc in range(8)])
         for j in range(8):
             out_ref[pl.ds((9 * rel + 8) * 8 + j, n, stride=288), :] = parts[j]
+        for f in range(n):
+            out_copy(rel, f).start()
+
+    def out_copy(rel, f):
+        rows = pl.ds((36 * f + 9 * rel) * 8, 72)
+        return pltpu.make_async_copy(out_ref.at[rows], result_ref.at[rows], o_sem.at[rel, f])
 
     own_b.wait()
     for odd in range(2):
@@ -497,6 +508,9 @@
                 @pl.when(lax.rem(r + k, 2) == odd)
                 def _():
                     b_copy(k, q, odd).wait_send()
+    for rel in range(4):
+        for f in range(FULL[rel]):
+            out_copy(rel, f).wait()
 
 
 def shards(ns, spectrum, ocean_mask, depth_class, freq_speed, coupling, source, gain_table):
@@ -505,9 +519,11 @@
     out = pl.pallas_call(
         functools.partial(kernel, ns),
         out_shape=jax.ShapeDtypeStruct((LOCAL * 8, 128), F32),
-        in_specs=[vmem, vmem, vmem, pl.BlockSpec(memory_space=pltpu.SMEM), hbm, hbm, vmem],
-        out_specs=vmem,
+        in_specs=[hbm, vmem, vmem, pl.BlockSpec(memory_space=pltpu.SMEM), hbm, hbm, vmem],
+        out_specs=hbm,
         scratch_shapes=[
+            pltpu.VMEM((LOCAL * 8, 128), F32),
+            pltpu.VMEM((LOCAL * 8, 128), F32),
             pltpu.VMEM((2, BINS, BINS), BF16),
             pltpu.VMEM((12, BINS, 256), BF16),
             pltpu.VMEM((12, 1536, 256), BF16),
@@ -526,6 +542,7 @@
             pltpu.VMEM((8, ROWS, 128), F32),
             pltpu.VMEM((8, ROWS, 128), F32),
             pltpu.VMEM((8, ROWS, 128), F32),
+            pltpu.VMEM((12, 4, 16, 128), F32),
             pltpu.VMEM((12, 4, 8, 128), F32),
             pltpu.VMEM((12, 8, 128), F32),
             pltpu.VMEM((PHASES, 12, 4, 16, 128), F32),
@@ -536,7 +553,7 @@
             pltpu.VMEM((128, 128), F32),
             pltpu.VMEM((8, 128), F32),
             pltpu.VMEM((2, 8, 128), F32),
-            dma((2,)), dma((8, 4)), dma((8, 4)), dma((8, 4)), dma((8, 4)), dma,
+            dma((2,)), dma((8, 4)), dma((8, 4)), dma((8, 4)), dma((8, 4)), dma, dma, dma((4, 5)),
             dma((PHASES, 4, 3)), dma((PHASES, 4, 3)), dma((2,)), dma((2,)),
         ],
         compiler_params=pltpu.CompilerParams(

time: 68.6 us -> 67.2 us (0.980)
  Pallas kernels: 66.4 us -> 65 us
    pallas_call x1, Pallas kernels: 66.4 us -> 65 us  [shards(): pl.pallas_call(functools.partial(kernel, ns), out_shape=jax.ShapeDtypeStr...]
where the time goes in v3:
time: 67.2 us; the launch traced here: 67 us
  Pallas kernels  65 us (97%)
  local copies, waits for them, and re-layouts  1.97 us (3%)
    pallas_call x1, Pallas kernels, shards(): pl.pallas_call(functools.partial(kernel, ns), out_shape=jax.ShapeDtypeStr...  65 us
    unnamed x1, local copies, waits for them, and re-layouts  1.97 us

profile of v3, /device:TPU:16, one launch (start us, length us, event | category | flops | bytes accessed | tf_op | source)
XLA Modules:
  0.0 67.0 jit_solution(11969897160151811217)
XLA Ops:
  0.0 65.0 %wave_steps.1 = f32[1296,128]{1,0:T(8,128)} custom-call(f32[1296,128]{1,0:T(8,128)} %bitcast.3, s32[8,128]{1,0:T(8,128)} %mask_ref.1, s32[8,128]{1,0:T(8,128)} %class_ref.1, f32[36]{0:T(128)} %speed_ref.1, bf16[1296,1296]{1,0:T(8,128)(2,1)} %coupling_ref.1, bf16[1296,1296]{1,0:T(8,128)(2,1)} %source_ref.1, f32[8,1296]{1,0:T(8,128)} %gain_ref.1), custom_call_target="tpu_custom_call" | custom-call | flops 12000000000 | bytes 9000000 | tf_op jit(solution)/shard_map/wave_steps/pallas_call | solution.py:519
  65.0 2.0 %copy.9 = f32[162,8,128]{2,1,0:T(8,128)} copy(f32[162,8,128]{2,1,0:T(8,128)} %bitcast.2) | data formatting | bytes 1327104

commit v4 on v3

--- a/solution.py
+++ b/solution.py
@@ -148,7 +148,7 @@
             src_ref=send_a.at[block_of(peer, half), rows], dst_ref=land_a.at[slot, rows],
             send_sem=a_send.at[k, rel], recv_sem=a_recv.at[slot, rel], device_id=(s, peer), device_id_type=MESH)
 
-    for rel in range(4):
+    for rel in QUADS:
         for k in range(1, NSPEC):
             a_copy(k, rel).start()
     own_a = pltpu.make_async_copy(send_a.at[c], land_a.at[r], own_sem)
@@ -223,15 +223,16 @@
 
     for copy in loads:
         copy.wait()
-    for m in range(2):
-        def columns(k, _, m=m):
-            rows = pl.ds(pl.multiple_of(432 * k, 16), 432)
-            for g in range(3):
-                total = to_quadrants(lambda at_, n: natural[m, rows, at_:at_ + n], g).astype(BF16)
-                for q in range(4):
-                    turned[3 * q + g, rows, 128 * m:128 * m + 128] = total[:, 128 * q:128 * q + 128]
-            return 0
-        lax.fori_loop(0, 3, columns, 0)
+    def columns(k, _):
+        m = k // 3
+        rows = pl.ds(pl.multiple_of(432 * lax.rem(k, 3), 16), 432)
+        lanes = pl.ds(pl.multiple_of(128 * m, 128), 128)
+        for g in range(3):
+            total = to_quadrants(lambda at_, n: natural[m, rows, at_:at_ + n], g).astype(BF16)
+            for q in range(4):
+                turned[3 * q + g, rows, lanes] = total[:, 128 * q:128 * q + 128]
+        return 0
+    lax.fori_loop(0, 6, columns, 0)
 
     for k, ds in ((0, -1), (1, 1)):
         @pl.when(there(0, ds))
@@ -375,9 +376,9 @@
     def second_half(qg):
         got = part[qg] + jnp.dot(xb[:, 768:], weights[qg, 768:, :], preferred_element_type=F32)
         change = gains[qg] * got[:, :128] + got[:, 128:]
-        slope[qg] = change
         js, is_ = interior(qg // 3)
         state = e0[qg, js, is_, :].reshape(128, 128)
+        slope[qg] = state + 0.5 * change
         yb[:, 128 * qg:128 * qg + 128] = (state + change).astype(BF16)
 
     def finish(q):
@@ -386,14 +387,13 @@
         for qg in range(3 * q, 3 * q + 3):
             got = jnp.dot(yb[...], weights[qg], preferred_element_type=F32)
             change = gains[qg] * got[:, :128] + got[:, 128:]
-            state = e0[qg, js, is_, :].reshape(128, 128)
-            e0[qg, js, is_, :] = (state + 0.5 * (slope[qg] + change)).reshape(8, 16, 128)
+            e0[qg, js, is_, :] = (slope[qg] + 0.5 * change).reshape(8, 16, 128)
 
     own_a.wait()
-    for rel in range(4):
-        for k in range(1, NSPEC):
-            a_copy(k, rel, incoming=True).wait_recv()
     for q in range(4):
+        for rel in ((0, 2), (), (1, 3), ())[q]:
+            for k in range(1, NSPEC):
+                a_copy(k, rel, incoming=True).wait_recv()
         for g in range(3):
             pieces = []
             for rr in range(NSPEC):

time: 67.2 us -> 66.9 us (level)
  no operation moved by 1% of the time
where the time goes in v4:
time: 66.9 us; the launch traced here: 66.7 us
  Pallas kernels  64.8 us (97%)
  local copies, waits for them, and re-layouts  1.97 us (3%)
    pallas_call x1, Pallas kernels, shards(): pl.pallas_call(functools.partial(kernel, ns), out_shape=jax.ShapeDtypeStr...  64.8 us
    unnamed x1, local copies, waits for them, and re-layouts  1.97 us

profile of v4, /device:TPU:16, one launch (start us, length us, event | category | flops | bytes accessed | tf_op | source)
XLA Modules:
  0.0 66.7 jit_solution(15836919079390546551)
XLA Ops:
  0.0 64.8 %wave_steps.1 = f32[1296,128]{1,0:T(8,128)} custom-call(f32[1296,128]{1,0:T(8,128)} %bitcast.3, s32[8,128]{1,0:T(8,128)} %mask_ref.1, s32[8,128]{1,0:T(8,128)} %class_ref.1, f32[36]{0:T(128)} %speed_ref.1, bf16[1296,1296]{1,0:T(8,128)(2,1)} %coupling_ref.1, bf16[1296,1296]{1,0:T(8,128)(2,1)} %source_ref.1, f32[8,1296]{1,0:T(8,128)} %gain_ref.1), custom_call_target="tpu_custom_call" | custom-call | flops 12000000000 | bytes 9000000 | tf_op jit(solution)/shard_map/wave_steps/pallas_call | solution.py:519
  64.8 2.0 %copy.9 = f32[162,8,128]{2,1,0:T(8,128)} copy(f32[162,8,128]{2,1,0:T(8,128)} %bitcast.2) | data formatting | bytes 1327104

commit v5 on v3

--- a/solution.py
+++ b/solution.py
@@ -300,12 +300,12 @@
                 cs[qg, at_:at_ + n, :] = e0[qg, j, ii:ii + n, :]
         start(2)
         for qg in groups:
-            ys[qg] = e0[qg, jy:jy + 4, off_i(q):off_i(q) + 16, :]
-        start(0)
-        for qg in groups:
             for j in range(8):
                 xs[qg, j // 2, 4 * (j % 2):4 * (j % 2) + 4, :] = e0[qg, off_j(q) + j, i:i + 4, :]
         start(1)
+        for qg in groups:
+            ys[qg] = e0[qg, jy:jy + 4, off_i(q):off_i(q) + 16, :]
+        start(0)
 
     def take_edges(p, q):
         i = 4 if LOWX[q] else 16

time: 67.2 us -> 67.2 us (level)
  no operation moved by 1% of the time
where the time goes in v5:
time: 67.2 us; the launch traced here: 67 us
  Pallas kernels  65 us (97%)
  local copies, waits for them, and re-layouts  1.97 us (3%)
    pallas_call x1, Pallas kernels, shards(): pl.pallas_call(functools.partial(kernel, ns), out_shape=jax.ShapeDtypeStr...  65 us
    unnamed x1, local copies, waits for them, and re-layouts  1.97 us

profile of v5, /device:TPU:16, one launch (start us, length us, event | category | flops | bytes accessed | tf_op | source)
XLA Modules:
  0.0 67.0 jit_solution(9263216147527292611)
XLA Ops:
  0.0 65.0 %wave_steps.1 = f32[1296,128]{1,0:T(8,128)} custom-call(f32[1296,128]{1,0:T(8,128)} %bitcast.3, s32[8,128]{1,0:T(8,128)} %mask_ref.1, s32[8,128]{1,0:T(8,128)} %class_ref.1, f32[36]{0:T(128)} %speed_ref.1, bf16[1296,1296]{1,0:T(8,128)(2,1)} %coupling_ref.1, bf16[1296,1296]{1,0:T(8,128)(2,1)} %source_ref.1, f32[8,1296]{1,0:T(8,128)} %gain_ref.1), custom_call_target="tpu_custom_call" | custom-call | flops 12000000000 | bytes 9000000 | tf_op jit(solution)/shard_map/wave_steps/pallas_call | solution.py:519
  65.0 2.0 %copy.9 = f32[162,8,128]{2,1,0:T(8,128)} copy(f32[162,8,128]{2,1,0:T(8,128)} %bitcast.2) | data formatting | bytes 1327104
